TPU v7x, 512 devices: a whole 4x4x16 slice. The times are simulated.
512 devices in a mesh: dp: 16 (over x_lo, y, core), expert: 32 (over x_hi, z).
Axes of the slice: x: 4 (x_hi: 2, x_lo: 2; x = x_hi * 2 + x_lo), y: 4, z: 16, core: 2. Of those that a mesh axis runs over, the one named last changes fastest.
Arguments:
- grad_out: bfloat16 [1024, 7168], P('expert', 'dp'), may hold values from -6 to 6
- routes: int32 [1024, 8], P('expert'), may hold values from 0 to 31, all different within a row; in each aligned block of 32 rows (0 to 31, 32 to 63, ...) at most 12 rows name the same one
- gates: float32 [1024, 8], P('expert'), may hold values from 0.05 to 1
- hidden: bfloat16 [32, 384, 2048], P('expert', None, 'dp'), may hold values from -0.1796875 to 0.1796875
- w_down: bfloat16 [32, 2048, 7168], P('expert', 'dp'), may hold values from -0.125 to 0.125
Outputs:
- d_hidden: bfloat16 [32, 384, 2048], P('expert', None, 'dp')
- d_down: bfloat16 [32, 2048, 7168], P('expert', 'dp')
- d_gate: float32 [1024, 8], P('expert')
Inputs may be any that keep to these rules, and one draw needn't show every extreme that they name: `routes`: each row names 8 different experts; within each aligned block of 32 rows (the tokens on one index of the expert axis) no expert is named by more than 12 rows.
All inputs are finite; a program needn't handle non-finite values.
Results may differ from a plain program's by a relative error of at most 0.0049.
Values may be sent and summed in bfloat16 or wider, within the bound.
No kernel may reach another device: no remote copies, remote signals or barrier semaphores. Data moves between devices by JAX's collectives and lax.ppermute only.
A program may use at most 128 MiB of HBM per device.

v0:
```python
import jax
import jax.numpy as jnp
from jax import lax
from jax.sharding import PartitionSpec as P


def route_tables(routes, gates, experts, capacity):
    tokens_here = routes.shape[0]
    expert_ids = lax.broadcasted_iota(jnp.int32, (1, 1, experts), 2)
    chosen = (routes[:, :, None] == expert_ids).astype(jnp.int32)
    present = jnp.sum(chosen, axis=1)
    before = jnp.cumsum(present, axis=0) - present
    route_rank = jnp.sum(chosen * before[:, None, :], axis=2)
    slot_ids = lax.broadcasted_iota(jnp.int32, (1, 1, 1, capacity), 3)
    placed = chosen[:, :, :, None] * (route_rank[:, :, None, None] == slot_ids).astype(jnp.int32)
    tok_index = lax.broadcasted_iota(jnp.int32, (tokens_here, 1, 1, 1), 0)
    slot_token = jnp.sum(placed * tok_index, axis=(0, 1))
    slot_gate = jnp.sum(placed.astype(jnp.float32) * gates[:, :, None, None], axis=(0, 1))
    counts = jnp.sum(present, axis=0)
    return (placed, slot_token, slot_gate, counts)


def on_device(grad_out, routes, gates, hidden, w_down):
    experts = lax.axis_size("expert")
    capacity = hidden.shape[1] // experts
    placed, slot_token, slot_gate, counts = route_tables(routes, gates, experts, capacity)
    picked = grad_out[slot_token]
    scaled = (slot_gate[:, :, None] * picked.astype(jnp.float32)).astype(jnp.bfloat16)
    arrived = lax.all_to_all(scaled, "expert", split_axis=0, concat_axis=0, tiled=True)
    arrived = lax.all_gather(arrived, "dp", axis=2, tiled=True)
    dispatched = arrived.reshape(-1, arrived.shape[2])
    activations = hidden[0]
    weight = w_down[0]
    values = lax.dot_general(
        dispatched, weight, (((1,), (1,)), ((), ())), preferred_element_type=jnp.float32
    )
    gate_terms = jnp.sum(activations.astype(jnp.float32) * values, axis=1)
    gradient = lax.dot_general(
        activations, dispatched, (((0,), (0,)), ((), ())), preferred_element_type=jnp.float32
    )
    d_hidden = values.astype(jnp.bfloat16)[None]
    d_down = gradient.astype(jnp.bfloat16)[None]
    summed = lax.psum(gate_terms, "dp")
    returned = lax.all_to_all(
        summed.reshape(experts, capacity), "expert", split_axis=0, concat_axis=0, tiled=True
    )
    matched = jnp.sum(placed.astype(jnp.float32) * returned[None, None, :, :], axis=(2, 3))
    d_gate = matched / gates
    return (d_hidden, d_down, d_gate)


def solution(mesh):
    in_specs = (
        P("expert", "dp"),
        P("expert", None),
        P("expert", None),
        P("expert", None, "dp"),
        P("expert", "dp", None),
    )
    out_specs = (P("expert", None, "dp"), P("expert", "dp", None), P("expert", None))
    return jax.shard_map(
        on_device, mesh=mesh, in_specs=in_specs, out_specs=out_specs, check_vma=False
    )
```

profile of v0, /device:TPU:2, one launch (start us, length us, event | category | flops | bytes accessed | tf_op | source)
XLA Modules:
  0.0 357.5 jit_solution(11881050243654104437)
XLA Ops:
  7.2 0.9 copy.26
  8.1 0.1 fusion.11
  8.4 0.7 select_reduce_fusion
  9.1 0.8 copy.27
  9.9 0.6 fusion.7
  10.5 0.6 fusion.5
  11.1 0.7 copy.28
  12.0 2.1 gather_fusion
  14.2 0.9 multiply_convert_fusion.1
  15.0 49.6 %all_to_all.14 = bf16[32,12,448]{2,1,0:T(8,128)(2,1)S(1)} all-to-all(bf16[32,12,448]{2,1,0:T(8,128)(2,1)S(1)} %multiply_convert_fusion.1), channel_id=1, replica_groups=mesh['dp'=16,'expert'=32] {'expert'}, dimensions={0} | all-to-all | bytes 688128 | tf_op jit(solution)/shard_map/all_to_all | solution.py:29
  64.6 2.2 copy.30
  66.8 0.1 copy.32
  66.9 150.9 %all-gather.2.cloned.1.call-done = bf16[32,12,7168]{0,1,2:T(8,128)(2,1)} async-done(((bf16[32,12,448]{0,1,2:T(8,128)(2,1)}), bf16[32,12,7168]{0,1,2:T(8,128)(2,1)}) %all-gather.2.cloned.1.call-update) | async-done | bytes 5505040 | tf_op jit(solution)/shard_map/all_gather | solution.py:30
  217.8 33.5 %copy.31 = bf16[32,12,7168]{2,1,0:T(8,128)(2,1)} copy(bf16[32,12,7168]{0,1,2:T(8,128)(2,1)} %all-gather.2.cloned.1.call-done) | data formatting | bytes 11010048 | tf_op jit(solution)/shard_map/all_gather | solution.py:30
  251.3 8.2 %reshape.54 = bf16[384,7168]{1,0:T(8,128)(2,1)} reshape(bf16[32,12,7168]{2,1,0:T(8,128)(2,1)} %copy.31) | data formatting | bytes 11010048 | tf_op jit(solution)/shard_map/reshape | solution.py:31
  259.5 4.3 %multiply_reduce_fusion = (f32[384]{0:T(512)S(1)}, bf16[1,384,128]{1,2,0:T(8,128)(2,1)S(1)}) fusion(bf16[1,384,128]{1,2,0:T(8,128)(2,1)S(1)} %copy.32, bf16[384,7168]{1,0:T(8,128)(2,1)} %reshape.54, bf16[1,128,7168]{2,1,0:T(8,128)(2,1)S(1)} %copy-done), kind=kOutput, calls=%fused_computation.15 | convolution fusion | flops 704839296 | bytes 7538176 | tf_op jit(solution)/shard_map/dot_general | solution.py:34
  263.9 56.3 %psum.7 = f32[32,1,12]{2,0,1:T(8,128)} all-reduce(f32[32,1,12]{2,0,1:T(8,128)S(1)} %all_to_all.10), channel_id=1, replica_groups=mesh['dp'=16,'expert'=32] {'dp'}, use_global_device_ids=true, to_apply=%region_6.7 | all-reduce | flops 384 | bytes 3072 | tf_op jit(solution)/shard_map/psum | solution.py:43
  320.2 14.1 %all-to-all-start.1 = ((f32[32,1,12]{2,1,0:T(1,128)}), f32[32,1,12]{2,1,0:T(1,128)S(1)}, u32[]{:S(2)}, u32[]{:S(2)}) async-start(f32[32,1,12]{2,1,0:T(1,128)} %bitcast.6), calls=%async_computation.1 | async-start | bytes 32768 | tf_op jit(solution)/shard_map/all_to_all | solution.py:44
  334.3 5.5 %fusion = bf16[1,128,7168]{1,2,0:T(8,128)(2,1)} fusion(bf16[384,7168]{1,0:T(8,128)(2,1)} %reshape.54, bf16[1,384,128]{2,1,0:T(8,128)(2,1)S(1)} %copy-done.4), kind=kOutput, calls=%fused_computation.2 | convolution fusion | flops 705560576 | bytes 7438336 | tf_op jit(solution)/shard_map/dot_general | solution.py:38
  339.8 0.8 copy.36
  340.6 3.9 %copy.37 = bf16[1,128,7168]{2,1,0:T(8,128)(2,1)} copy(bf16[1,128,7168]{1,2,0:T(8,128)(2,1)} %fusion) | data formatting | bytes 3670016
  344.5 4.5 %all-to-all-done.1 = f32[32,1,12]{2,1,0:T(1,128)S(1)} async-done(((f32[32,1,12]{2,1,0:T(1,128)}), f32[32,1,12]{2,1,0:T(1,128)S(1)}, u32[]{:S(2)}, u32[]{:S(2)}) %all-to-all-start.1) | async-done | bytes 1568 | tf_op jit(solution)/shard_map/all_to_all | solution.py:44
  349.1 0.9 fusion.6
  349.9 0.7 copy.38
  (24 shorter events, 0.7 us)
Async XLA Ops:
  7.2 252.4 %copy-start = (bf16[1,128,7168]{2,1,0:T(8,128)(2,1)S(1)}, bf16[1,128,7168]{2,1,0:T(8,128)(2,1)}, u32[]{:S(2)}) copy-start(bf16[1,128,7168]{2,1,0:T(8,128)(2,1)} %param.9) | copy-start | bytes 5505028
  7.2 4.8 %copy-start.1 = (bf16[32,448]{1,0:T(8,128)(2,1)S(1)}, bf16[32,448]{1,0:T(8,128)(2,1)}, u32[]{:S(2)}) copy-start(bf16[32,448]{1,0:T(8,128)(2,1)} %param.5) | copy-start | bytes 86020
  7.2 210.6 %all-gather.2.cloned.1.call-start = ((), (), s32[]{:S(2)}) async-start(), calls=%async_computation.2 | async-start | bytes 31195136 | tf_op jit(solution)/shard_map/all_gather | solution.py:30
  8.3 3.7 %copy-start.2 = (s32[32,8,32]{2,1,0:T(8,128)}, s32[32,8,32]{2,1,0:T(8,128)S(1)}, u32[]{:S(2)}) copy-start(s32[32,8,32]{2,1,0:T(8,128)S(1)} %fusion.9) | copy-start | bytes 98308
  64.6 2.2 copy-start.4
  320.2 28.7 %all-to-all-start.1 = ((f32[32,1,12]{2,1,0:T(1,128)}), f32[32,1,12]{2,1,0:T(1,128)S(1)}, u32[]{:S(2)}, u32[]{:S(2)}) async-start(f32[32,1,12]{2,1,0:T(1,128)} %bitcast.6), calls=%async_computation.1 | async-start | bytes 32768 | tf_op jit(solution)/shard_map/all_to_all | solution.py:44
  340.6 8.5 %copy-start.3 = (s32[32,8,32]{2,1,0:T(8,128)S(1)}, s32[32,8,32]{2,1,0:T(8,128)}, u32[]{:S(2)}) copy-start(s32[32,8,32]{2,1,0:T(8,128)} %copy-done.2) | copy-start | bytes 98308
Sparse Core Ops, SparseCore 0:
  66.9 150.8 all-gather.1
where the time goes:
time: 359 us; the launch traced here: 357 us
  waiting for transfers between devices  155 us (43%)
  blocking collectives  106 us (30%)
  local copies, waits for them, and re-layouts  54.2 us (15%)
  between operations  14.2 us (4%)
  starting transfers between devices  14.1 us (4%)
  matrix products  9.79 us (3%)
  other arithmetic  3.91 us (1%)
    all_gather x1, waiting for transfers between devices, on_device(): arrived = lax.all_gather(arrived, 'dp', axis=2, tiled=True)  151 us
    psum x1, blocking collectives, on_device(): summed = lax.psum(gate_terms, 'dp')  56.3 us
    all_to_all x1, blocking collectives, on_device(): lax.all_to_all(scaled, 'expert', split_axis=0, concat_axis=0, tiled=True)  49.6 us
    all_gather x1, local copies, waits for them, and re-layouts, on_device(): arrived = lax.all_gather(arrived, 'dp', axis=2, tiled=True)  33.5 us
    all_to_all x1, starting transfers between devices, on_device(): lax.all_to_all(summed.reshape(experts, capacity), 'expert', split_axis=0,...  14.1 us
    reshape x1, local copies, waits for them, and re-layouts, on_device(): dispatched = arrived.reshape(-1, arrived.shape[2])  8.24 us
  transfers between devices with their start and end apart: 2, of which 2 were waited for; matrix products, arithmetic and copies ran while one was open for 3% of the time, Pallas kernels for 0%

commit v1 on v0

--- a/solution.py
+++ b/solution.py
@@ -27,7 +27,9 @@
     picked = grad_out[slot_token]
     scaled = (slot_gate[:, :, None] * picked.astype(jnp.float32)).astype(jnp.bfloat16)
     arrived = lax.all_to_all(scaled, "expert", split_axis=0, concat_axis=0, tiled=True)
-    arrived = lax.all_gather(arrived, "dp", axis=2, tiled=True)
+    arrived = jnp.concatenate(
+        lax.all_to_all(jnp.stack([arrived] * lax.axis_size("dp")), "dp", 0, 0), axis=2
+    )
     dispatched = arrived.reshape(-1, arrived.shape[2])
     activations = hidden[0]
     weight = w_down[0]

time: 359 us -> 265 us (0.74)
  waiting for transfers between devices: 155 us -> 91.1 us
  local copies, waits for them, and re-layouts: 54.2 us -> 34 us
  between operations: 14.2 us -> 0.78 us
  blocking collectives: 106 us -> 113 us
    all_gather x1 -> x0, waiting for transfers between devices: 151 us -> none  [on_device(): arrived = lax.all_gather(arrived, 'dp', axis=2, tiled=True)]
    all_to_all x0 -> x1, waiting for transfers between devices: none -> 86.8 us  [on_device(): lax.all_to_all(jnp.stack([arrived] * lax.axis_size('dp')), 'dp', 0, 0)]
    all_gather x1 -> x0, local copies, waits for them, and re-layouts: 33.5 us -> none  [on_device(): arrived = lax.all_gather(arrived, 'dp', axis=2, tiled=True)]
    another operation x0 -> x2, local copies, waits for them, and re-layouts: none -> 14.5 us  [the longest x1 11 us: on_device(): dispatched = arrived.reshape(-1, arrived.shape[2])]
    all_to_all x1, starting transfers between devices: 14.1 us -> 5.37 us  [on_device(): lax.all_to_all(summed.reshape(experts, capacity), 'expert', split_axis=0,...]
    psum x1, blocking collectives: 56.3 us -> 63.6 us  [on_device(): summed = lax.psum(gate_terms, 'dp')]
    all_to_all x0 -> x1, starting transfers between devices: none -> 6.08 us  [on_device(): lax.all_to_all(jnp.stack([arrived] * lax.axis_size('dp')), 'dp', 0, 0)]
  transfers between devices with their start and end apart: 2 -> 2, of which waited for: 2 -> 2; matrix products, arithmetic and copies ran while one was open for 3% -> 4% of each run, Pallas kernels for 0% -> 0%
where the time goes in v1:
time: 265 us; the launch traced here: 264 us
  blocking collectives  113 us (43%)
  waiting for transfers between devices  91.1 us (34%)
  local copies, waits for them, and re-layouts  34 us (13%)
  starting transfers between devices  11.4 us (4%)
  matrix products  9.79 us (4%)
  other arithmetic  3.91 us (1%)
    all_to_all x1, waiting for transfers between devices, on_device(): lax.all_to_all(jnp.stack([arrived] * lax.axis_size('dp')), 'dp', 0, 0)  86.8 us
    psum x1, blocking collectives, on_device(): summed = lax.psum(gate_terms, 'dp')  63.6 us
    all_to_all x1, blocking collectives, on_device(): lax.all_to_all(scaled, 'expert', split_axis=0, concat_axis=0, tiled=True)  49.6 us
    another operation x1, local copies, waits for them, and re-layouts, on_device(): dispatched = arrived.reshape(-1, arrived.shape[2])  11 us
    reshape x1, local copies, waits for them, and re-layouts, on_device(): jnp.concatenate(lax.all_to_all(jnp.stack([arrived] * lax.axis_size('dp'))...  8.98 us
    unnamed x16, local copies, waits for them, and re-layouts  7.14 us
    all_to_all x1, starting transfers between devices, on_device(): lax.all_to_all(jnp.stack([arrived] * lax.axis_size('dp')), 'dp', 0, 0)  6.08 us
    dot_general x1, matrix products, on_device(): lax.dot_general(activations, dispatched, (((0,), (0,)), ((), ())), prefer...  5.49 us
  transfers between devices with their start and end apart: 2, of which 2 were waited for; matrix products, arithmetic and copies ran while one was open for 4% of the time, Pallas kernels for 0%

profile of v1, /device:TPU:2, one launch (start us, length us, event | category | flops | bytes accessed | tf_op | source)
XLA Modules:
  0.0 264.2 jit_solution(4878744424610562011)
XLA Ops:
  0.7 0.9 copy.33
  1.9 0.7 select_reduce_fusion
  2.6 0.8 copy.34
  3.3 0.6 fusion.7
  3.9 0.6 fusion.5
  4.5 0.7 copy.35
  5.5 2.1 gather_fusion
  7.6 0.9 multiply_convert_fusion.1
  8.5 49.6 %all_to_all.19 = bf16[32,12,448]{2,1,0:T(8,128)(2,1)S(1)} all-to-all(bf16[32,12,448]{2,1,0:T(8,128)(2,1)S(1)} %multiply_convert_fusion.1), channel_id=1, replica_groups=mesh['dp'=16,'expert'=32] {'expert'}, dimensions={0} | all-to-all | bytes 688128 | tf_op jit(solution)/shard_map/all_to_all | solution.py:29
  58.0 0.2 copy.37
  58.3 3.4 %stack.2 = bf16[16,32,12,448]{3,1,2,0:T(8,128)(2,1)} broadcast(bf16[32,12,448]{2,0,1:T(8,128)(2,1)S(1)} %copy.37), dimensions={1,2,3} | broadcast | bytes 5849088 | tf_op jit(solution)/shard_map/stack | solution.py:31
  61.7 6.1 %all-to-all-start.1 = ((bf16[16,32,12,448]{3,1,2,0:T(8,128)(2,1)}), bf16[16,32,12,448]{3,1,2,0:T(8,128)(2,1)}, u32[]{:S(2)}, u32[]{:S(2)}) async-start(bf16[16,32,12,448]{3,1,2,0:T(8,128)(2,1)} %stack.2), calls=%async_computation.1 | async-start | bytes 12582912 | tf_op jit(solution)/shard_map/all_to_all | solution.py:31
  67.9 86.8 %all-to-all-done.1 = bf16[16,32,12,448]{3,1,2,0:T(8,128)(2,1)} async-done(((bf16[16,32,12,448]{3,1,2,0:T(8,128)(2,1)}), bf16[16,32,12,448]{3,1,2,0:T(8,128)(2,1)}, u32[]{:S(2)}, u32[]{:S(2)}) %all-to-all-start.1) | async-done | bytes 5505056 | tf_op jit(solution)/shard_map/all_to_all | solution.py:31
  154.7 9.0 %copy.38 = bf16[32,12,16,448]{3,2,1,0:T(8,128)(2,1)} copy(bf16[32,12,16,448]{3,0,1,2:T(8,128)(2,1)} %bitcast.1) | data formatting | bytes 11010048 | tf_op jit(solution)/shard_map/reshape | solution.py:30
  163.7 11.0 %reshape_reshape.3 = bf16[384,7168]{1,0:T(8,128)(2,1)} reshape(bf16[32,12,16,448]{3,2,1,0:T(8,128)(2,1)} %copy.38) | data formatting | bytes 11010048 | tf_op jit(solution)/shard_map/reshape;reshape | solution.py:33
  174.7 4.3 %multiply_reduce_fusion = (f32[384]{0:T(512)S(1)}, bf16[1,384,128]{1,2,0:T(8,128)(2,1)S(1)}) fusion(bf16[1,384,128]{1,2,0:T(8,128)(2,1)S(1)} %copy.39, bf16[384,7168]{1,0:T(8,128)(2,1)} %reshape_reshape.3, bf16[1,128,7168]{2,1,0:T(8,128)(2,1)S(1)} %copy-done), kind=kOutput, calls=%fused_computation.15 | convolution fusion | flops 704839296 | bytes 7538176 | tf_op jit(solution)/shard_map/dot_general | solution.py:36
  179.1 63.6 %psum.7 = f32[32,1,12]{2,0,1:T(8,128)} all-reduce(f32[32,1,12]{2,0,1:T(8,128)S(1)} %all_to_all.14), channel_id=1, replica_groups=mesh['dp'=16,'expert'=32] {'dp'}, use_global_device_ids=true, to_apply=%region_6.7 | all-reduce | flops 384 | bytes 3072 | tf_op jit(solution)/shard_map/psum | solution.py:45
  242.7 5.4 %all-to-all-start.2 = ((f32[32,1,12]{2,1,0:T(1,128)}), f32[32,1,12]{2,1,0:T(1,128)S(1)}, u32[]{:S(2)}, u32[]{:S(2)}) async-start(f32[32,1,12]{2,1,0:T(1,128)} %bitcast.7), calls=%async_computation.2 | async-start | bytes 32768 | tf_op jit(solution)/shard_map/all_to_all | solution.py:46
  248.1 5.5 %fusion = bf16[1,128,7168]{1,2,0:T(8,128)(2,1)} fusion(bf16[384,7168]{1,0:T(8,128)(2,1)} %reshape_reshape.3, bf16[1,384,128]{2,1,0:T(8,128)(2,1)S(1)} %copy-done.4), kind=kOutput, calls=%fused_computation.2 | convolution fusion | flops 705560576 | bytes 7438336 | tf_op jit(solution)/shard_map/dot_general | solution.py:40
  253.6 0.8 copy.43
  254.3 3.9 %copy.44 = bf16[1,128,7168]{2,1,0:T(8,128)(2,1)} copy(bf16[1,128,7168]{1,2,0:T(8,128)(2,1)} %fusion) | data formatting | bytes 3670016
  258.3 4.3 %all-to-all-done.2 = f32[32,1,12]{2,1,0:T(1,128)S(1)} async-done(((f32[32,1,12]{2,1,0:T(1,128)}), f32[32,1,12]{2,1,0:T(1,128)S(1)}, u32[]{:S(2)}, u32[]{:S(2)}) %all-to-all-start.2) | async-done | bytes 1568 | tf_op jit(solution)/shard_map/all_to_all | solution.py:46
  262.7 0.9 fusion.6
  263.5 0.7 copy.45
  (24 shorter events, 0.9 us)
Async XLA Ops:
  0.6 174.1 %copy-start = (bf16[1,128,7168]{2,1,0:T(8,128)(2,1)S(1)}, bf16[1,128,7168]{2,1,0:T(8,128)(2,1)}, u32[]{:S(2)}) copy-start(bf16[1,128,7168]{2,1,0:T(8,128)(2,1)} %param.9) | copy-start | bytes 5505028
  0.6 4.8 %copy-start.1 = (bf16[32,448]{1,0:T(8,128)(2,1)S(1)}, bf16[32,448]{1,0:T(8,128)(2,1)}, u32[]{:S(2)}) copy-start(bf16[32,448]{1,0:T(8,128)(2,1)} %param.5) | copy-start | bytes 86020
  1.8 3.7 %copy-start.2 = (s32[32,8,32]{2,1,0:T(8,128)}, s32[32,8,32]{2,1,0:T(8,128)S(1)}, u32[]{:S(2)}) copy-start(s32[32,8,32]{2,1,0:T(8,128)S(1)} %fusion.9) | copy-start | bytes 98308
  61.7 6.1 %copy-start.4 = (bf16[1,384,128]{2,1,0:T(8,128)(2,1)S(1)}, bf16[1,384,128]{2,1,0:T(8,128)(2,1)}, u32[]{:S(2)}) copy-start(bf16[1,384,128]{2,1,0:T(8,128)(2,1)} %param.8) | copy-start | bytes 294916
  61.7 93.0 %all-to-all-start.1 = ((bf16[16,32,12,448]{3,1,2,0:T(8,128)(2,1)}), bf16[16,32,12,448]{3,1,2,0:T(8,128)(2,1)}, u32[]{:S(2)}, u32[]{:S(2)}) async-start(bf16[16,32,12,448]{3,1,2,0:T(8,128)(2,1)} %stack.2), calls=%async_computation.1 | async-start | bytes 12582912 | tf_op jit(solution)/shard_map/all_to_all | solution.py:31
  242.7 19.8 %all-to-all-start.2 = ((f32[32,1,12]{2,1,0:T(1,128)}), f32[32,1,12]{2,1,0:T(1,128)S(1)}, u32[]{:S(2)}, u32[]{:S(2)}) async-start(f32[32,1,12]{2,1,0:T(1,128)} %bitcast.7), calls=%async_computation.2 | async-start | bytes 32768 | tf_op jit(solution)/shard_map/all_to_all | solution.py:46
  254.3 8.3 %copy-start.3 = (s32[32,8,32]{2,1,0:T(8,128)S(1)}, s32[32,8,32]{2,1,0:T(8,128)}, u32[]{:S(2)}) copy-start(s32[32,8,32]{2,1,0:T(8,128)} %copy-done.2) | copy-start | bytes 98308

commit v2 on v0

--- a/solution.py
+++ b/solution.py
@@ -40,7 +40,7 @@
     )
     d_hidden = values.astype(jnp.bfloat16)[None]
     d_down = gradient.astype(jnp.bfloat16)[None]
-    summed = lax.psum(gate_terms, "dp")
+    summed = jnp.sum(lax.all_gather(gate_terms, "dp"), axis=0)
     returned = lax.all_to_all(
         summed.reshape(experts, capacity), "expert", split_axis=0, concat_axis=0, tiled=True
     )

time: 359 us -> 323 us (0.90)
  the two profiles are of different devices: /device:TPU:2 before, /device:TPU:1 now
where the time goes in v2:
time: 323 us; the launch traced here: 322 us
  waiting for transfers between devices  155 us (48%)
  blocking collectives  69.5 us (22%)
  local copies, waits for them, and re-layouts  54.8 us (17%)
  starting transfers between devices  14.5 us (4%)
  between operations  14.2 us (4%)
  matrix products  9.79 us (3%)
  other arithmetic  3.95 us (1%)
    all_gather x1, waiting for transfers between devices, on_device(): arrived = lax.all_gather(arrived, 'dp', axis=2, tiled=True)  152 us
    all_to_all x1, blocking collectives, on_device(): lax.all_to_all(scaled, 'expert', split_axis=0, concat_axis=0, tiled=True)  50.5 us
    all_gather x1, local copies, waits for them, and re-layouts, on_device(): arrived = lax.all_gather(arrived, 'dp', axis=2, tiled=True)  33.5 us
    all_gather x1, blocking collectives, on_device(): summed = jnp.sum(lax.all_gather(gate_terms, 'dp'), axis=0)  19 us
    all_to_all x1, starting transfers between devices, on_device(): lax.all_to_all(summed.reshape(experts, capacity), 'expert', split_axis=0,...  14.4 us
    reshape x1, local copies, waits for them, and re-layouts, on_device(): dispatched = arrived.reshape(-1, arrived.shape[2])  8.24 us
    unnamed x17, local copies, waits for them, and re-layouts  7.13 us
  transfers between devices with their start and end apart: 2, of which 2 were waited for; matrix products, arithmetic and copies ran while one was open for 3% of the time, Pallas kernels for 0%

profile of v2, /device:TPU:1, one launch (start us, length us, event | category | flops | bytes accessed | tf_op | source)
XLA Modules:
  0.0 321.8 jit_solution(14951855450177900520)
XLA Ops:
  7.2 0.9 copy.26
  8.4 0.7 select_reduce_fusion
  9.1 0.8 copy.27
  9.9 0.6 fusion.7
  10.5 0.6 fusion.5
  11.1 0.7 copy.28
  12.0 2.1 gather_fusion
  14.2 0.9 multiply_convert_fusion.1
  15.0 50.5 %all_to_all.14 = bf16[32,12,448]{2,1,0:T(8,128)(2,1)S(1)} all-to-all(bf16[32,12,448]{2,1,0:T(8,128)(2,1)S(1)} %multiply_convert_fusion.1), channel_id=1, replica_groups=mesh['dp'=16,'expert'=32] {'expert'}, dimensions={0} | all-to-all | bytes 688128 | tf_op jit(solution)/shard_map/all_to_all | solution.py:29
  65.5 2.2 copy.30
  67.7 0.1 copy.32
  67.8 151.6 %all-gather.4.cloned.1.call-done = bf16[32,12,7168]{0,1,2:T(8,128)(2,1)} async-done(((bf16[32,12,448]{0,1,2:T(8,128)(2,1)}), bf16[32,12,7168]{0,1,2:T(8,128)(2,1)}) %all-gather.4.cloned.1.call-update) | async-done | bytes 5505040 | tf_op jit(solution)/shard_map/all_gather | solution.py:30
  219.4 33.5 %copy.31 = bf16[32,12,7168]{2,1,0:T(8,128)(2,1)} copy(bf16[32,12,7168]{0,1,2:T(8,128)(2,1)} %all-gather.4.cloned.1.call-done) | data formatting | bytes 11010048 | tf_op jit(solution)/shard_map/all_gather | solution.py:30
  252.9 8.2 %reshape.54 = bf16[384,7168]{1,0:T(8,128)(2,1)} reshape(bf16[32,12,7168]{2,1,0:T(8,128)(2,1)} %copy.31) | data formatting | bytes 11010048 | tf_op jit(solution)/shard_map/reshape | solution.py:31
  261.1 4.3 %multiply_reduce_fusion = (f32[384]{0:T(512)S(1)}, bf16[1,384,128]{1,2,0:T(8,128)(2,1)S(1)}) fusion(bf16[1,384,128]{1,2,0:T(8,128)(2,1)S(1)} %copy.32, bf16[384,7168]{1,0:T(8,128)(2,1)} %reshape.54, bf16[1,128,7168]{2,1,0:T(8,128)(2,1)S(1)} %copy-done), kind=kOutput, calls=%fused_computation.15 | convolution fusion | flops 704839296 | bytes 7538176 | tf_op jit(solution)/shard_map/dot_general | solution.py:34
  265.4 19.0 %all-gather.1 = f32[16,1,384]{2,1,0:T(1,128)S(1)} all-gather(f32[1,1,384]{2,1,0:T(1,128)S(1)} %reshape.66), channel_id=2, replica_groups=mesh['dp'=16,'expert'=32] {'dp'}, dimensions={0}, use_global_device_ids=true | all-gather | bytes 26112 | tf_op jit(solution)/shard_map/all_gather | solution.py:43
  284.5 0.7 all_to_all.10
  285.2 14.4 %all-to-all-start.1 = ((f32[32,1,12]{2,1,0:T(1,128)}), f32[32,1,12]{2,1,0:T(1,128)S(1)}, u32[]{:S(2)}, u32[]{:S(2)}) async-start(f32[32,1,12]{2,1,0:T(1,128)} %bitcast.6), calls=%async_computation.1 | async-start | bytes 32768 | tf_op jit(solution)/shard_map/all_to_all | solution.py:44
  299.6 5.5 %fusion = bf16[1,128,7168]{1,2,0:T(8,128)(2,1)} fusion(bf16[384,7168]{1,0:T(8,128)(2,1)} %reshape.54, bf16[1,384,128]{2,1,0:T(8,128)(2,1)S(1)} %copy-done.4), kind=kOutput, calls=%fused_computation.2 | convolution fusion | flops 705560576 | bytes 7438336 | tf_op jit(solution)/shard_map/dot_general | solution.py:38
  305.1 0.8 copy.36
  305.9 3.9 %copy.37 = bf16[1,128,7168]{2,1,0:T(8,128)(2,1)} copy(bf16[1,128,7168]{1,2,0:T(8,128)(2,1)} %fusion) | data formatting | bytes 3670016
  309.8 3.5 %all-to-all-done.1 = f32[32,1,12]{2,1,0:T(1,128)S(1)} async-done(((f32[32,1,12]{2,1,0:T(1,128)}), f32[32,1,12]{2,1,0:T(1,128)S(1)}, u32[]{:S(2)}, u32[]{:S(2)}) %all-to-all-start.1) | async-done | bytes 1568 | tf_op jit(solution)/shard_map/all_to_all | solution.py:44
  313.4 0.9 fusion.6
  314.3 0.7 copy.38
  (26 shorter events, 0.8 us)
Async XLA Ops:
  7.2 254.0 %copy-start = (bf16[1,128,7168]{2,1,0:T(8,128)(2,1)S(1)}, bf16[1,128,7168]{2,1,0:T(8,128)(2,1)}, u32[]{:S(2)}) copy-start(bf16[1,128,7168]{2,1,0:T(8,128)(2,1)} %param.9) | copy-start | bytes 5505028
  7.2 4.8 %copy-start.1 = (bf16[32,448]{1,0:T(8,128)(2,1)S(1)}, bf16[32,448]{1,0:T(8,128)(2,1)}, u32[]{:S(2)}) copy-start(bf16[32,448]{1,0:T(8,128)(2,1)} %param.5) | copy-start | bytes 86020
  7.2 212.2 %all-gather.4.cloned.1.call-start = ((), (), s32[]{:S(2)}) async-start(), calls=%async_computation.2 | async-start | bytes 31195136 | tf_op jit(solution)/shard_map/all_gather | solution.py:30
  8.3 3.7 %copy-start.2 = (s32[32,8,32]{2,1,0:T(8,128)}, s32[32,8,32]{2,1,0:T(8,128)S(1)}, u32[]{:S(2)}) copy-start(s32[32,8,32]{2,1,0:T(8,128)S(1)} %fusion.9) | copy-start | bytes 98308
  65.5 2.2 copy-start.4
  285.2 28.1 %all-to-all-start.1 = ((f32[32,1,12]{2,1,0:T(1,128)}), f32[32,1,12]{2,1,0:T(1,128)S(1)}, u32[]{:S(2)}, u32[]{:S(2)}) async-start(f32[32,1,12]{2,1,0:T(1,128)} %bitcast.6), calls=%async_computation.1 | async-start | bytes 32768 | tf_op jit(solution)/shard_map/all_to_all | solution.py:44
  305.9 7.5 %copy-start.3 = (s32[32,8,32]{2,1,0:T(8,128)S(1)}, s32[32,8,32]{2,1,0:T(8,128)}, u32[]{:S(2)}) copy-start(s32[32,8,32]{2,1,0:T(8,128)} %copy-done.2) | copy-start | bytes 98308
Sparse Core Ops, SparseCore 0:
  67.8 151.5 all-gather.3
